TPU v7x, 32 devices: a whole 2x2x4 slice. The times are simulated.
32 devices in a mesh: groups: 2 (over y), dp: 4 (over z), tensor: 4 (over x, core).
Axes of the slice: x: 2, y: 2, z: 4, core: 2. Of those that a mesh axis runs over, the one named last changes fastest.
Arguments:
- query: bfloat16 [4, 32, 64, 128], P(None, ('groups', 'dp'), 'tensor'), parts along dimension 1, may hold values from -72 to 72
- new_kv: bfloat16 [4, 32, 8, 256], P(None, ('groups', 'dp'), 'tensor'), parts along dimension 1, may hold values from -18 to 18
- tail_pool: bfloat16 [64, 4, 8, 256], P(('groups', 'dp'), None, 'tensor'), parts along dimension 0, may hold values from -18 to 18
- page_table: int32 [32, 2], P(('groups', 'dp')), parts along dimension 0, may hold values from 0 to 7, as said below
- tail_len: int32 [32], P(('groups', 'dp')), parts along dimension 0, may hold values from 1 to 4, as said below
- fork_parent: int32 [4, 32], P(None, 'groups'), parts along dimension 1, may hold values from -1 to 15, as said below
- prompt_kv: bfloat16 [4096, 8, 256], P('groups', 'tensor'), parts along dimension 0, may hold values from -6 to 6
- out_weight: bfloat16 [8192, 8192], P('tensor', 'dp'), may hold values from -0.0625 to 0.0625
- residual: bfloat16 [4, 32, 8192], P(None, ('groups', 'tensor'), 'dp'), parts along dimension 1, may hold values from -1.5 to 1.5
Outputs:
- mixed: bfloat16 [4, 32, 8192], P(None, ('groups', 'tensor'), 'dp'), parts along dimension 1
There are 2 independent parts, one for each index of `groups`. A program takes and returns all parts, laid end to end along the dimension named above; an argument that names none is the same for every part. Nothing has to cross between parts.
Inputs may be any that keep to these rules, and one draw needn't show every extreme that they name: `page_table`: for each node's owner, the rows of the nodes of one index of dp form a permutation of 0 to 7. `tail_len`: some node has exactly 4 tokens. `fork_parent`: at each step every index of dp holds exactly one node with a value other than -1, and all values that name nodes of one index of dp at one step name the same node.
All inputs are finite; a program needn't handle non-finite values.
Results may differ from a plain program's by a relative error of at most 0.013.
Values may be sent and summed in bfloat16 or wider, within the bound.
A program may use at most 64 MiB of HBM per device.

v0:
```python
import jax
import jax.numpy as jnp
from jax import lax
from jax.sharding import PartitionSpec as P


def local(
    query, new_kv, tail_pool, page_table, tail_len, fork_parent, prompt_kv, out_weight, residual
):
    steps_count = query.shape[0]
    local_nodes = query.shape[1]
    local_heads = query.shape[2]
    head_dim = query.shape[3]
    kv_local = prompt_kv.shape[1]
    group_size = local_heads // kv_local
    tail_tokens = tail_pool.shape[1] * page_table.shape[1]
    score_scale = head_dim ** (-0.5)
    node_base = lax.axis_index("dp") * local_nodes
    tail_cache = tail_pool[page_table.reshape(-1)].reshape(
        local_nodes, tail_tokens, kv_local, 2 * head_dim
    )
    tail_lengths = tail_len
    query_rows = query.reshape(steps_count, local_nodes, kv_local, group_size, head_dim)
    query_rows = query_rows.transpose(2, 0, 1, 3, 4).reshape(kv_local, -1, head_dim)
    prompt_scores = (
        jnp.einsum(
            "krd,pkd->krp",
            query_rows,
            prompt_kv[..., :head_dim],
            preferred_element_type=jnp.float32,
        )
        * score_scale
    )
    prompt_max = prompt_scores.max(-1)
    prompt_weights = jnp.exp(prompt_scores - prompt_max[..., None])
    prompt_sum = prompt_weights.sum(-1)
    prompt_acc = jnp.einsum(
        "krp,pkd->krd",
        prompt_weights.astype(jnp.bfloat16),
        prompt_kv[..., head_dim:],
        preferred_element_type=jnp.float32,
    )
    prompt_max = prompt_max.reshape(kv_local, steps_count, local_nodes, group_size).transpose(
        1, 2, 0, 3
    )
    prompt_sum = prompt_sum.reshape(kv_local, steps_count, local_nodes, group_size).transpose(
        1, 2, 0, 3
    )
    prompt_acc = prompt_acc.reshape(
        kv_local, steps_count, local_nodes, group_size, head_dim
    ).transpose(1, 2, 0, 3, 4)
    positions = jnp.arange(tail_tokens, dtype=jnp.int32)
    head_list = []
    for moment in range(steps_count):
        parents = fork_parent[moment]
        relative = parents - node_base
        exported = (relative >= 0) & (relative < local_nodes)
        export_index = jnp.max(jnp.where(exported, relative, 0))
        export_tail = lax.dynamic_slice_in_dim(tail_cache, export_index, 1, 0)
        export_length = lax.dynamic_slice_in_dim(tail_lengths, export_index, 1, 0).astype(
            jnp.bfloat16
        )
        got_tails, got_lengths = (
            lax.all_gather(export_tail, "dp", axis=0, tiled=True),
            lax.all_gather(export_length, "dp", axis=0, tiled=True),
        )
        own_parents = lax.dynamic_slice_in_dim(parents, node_base, local_nodes, 0)
        forked = own_parents >= 0
        source_device = jnp.where(forked, own_parents // local_nodes, 0)
        fetched = got_tails[source_device]
        fetched_lengths = got_lengths[source_device].astype(jnp.int32)
        tail_cache = jnp.where(forked[:, None, None, None], fetched, tail_cache)
        tail_lengths = jnp.where(forked, fetched_lengths, tail_lengths)
        landing = positions[None, :] == tail_lengths[:, None]
        tail_cache = jnp.where(landing[:, :, None, None], new_kv[moment][:, None], tail_cache)
        visible = positions[None, :] <= tail_lengths[:, None]
        step_queries = query[moment].reshape(local_nodes, kv_local, group_size, head_dim)
        tail_scores = (
            jnp.einsum(
                "nkgd,ntkd->nkgt",
                step_queries,
                tail_cache[..., :head_dim],
                preferred_element_type=jnp.float32,
            )
            * score_scale
        )
        tail_scores = jnp.where(visible[:, None, None, :], tail_scores, -jnp.inf)
        step_max = prompt_max[moment]
        highest = jnp.maximum(step_max, tail_scores.max(-1))
        tail_weights = jnp.exp(tail_scores - highest[..., None])
        carried = jnp.exp(step_max - highest)
        denominator = prompt_sum[moment] * carried + tail_weights.sum(-1)
        mixed_values = prompt_acc[moment] * carried[..., None] + jnp.einsum(
            "nkgt,ntkd->nkgd",
            tail_weights.astype(jnp.bfloat16),
            tail_cache[..., head_dim:],
            preferred_element_type=jnp.float32,
        )
        head_list.append(
            (mixed_values / denominator[..., None])
            .reshape(local_nodes, local_heads * head_dim)
            .astype(jnp.bfloat16)
        )
        tail_lengths = tail_lengths + 1
    head_outputs = jnp.stack(head_list)
    projected = jnp.einsum(
        "snf,fc->snc",
        lax.all_gather(head_outputs, "dp", axis=1, tiled=True),
        out_weight,
        preferred_element_type=jnp.float32,
    )
    summed = lax.psum_scatter(
        projected.astype(jnp.bfloat16), "tensor", scatter_dimension=1, tiled=True
    ).astype(jnp.float32)
    return (residual.astype(jnp.float32) + summed).astype(jnp.bfloat16)


def solution(mesh):
    in_specs = (
        P(None, ("groups", "dp"), "tensor", None),
        P(None, ("groups", "dp"), "tensor", None),
        P(("groups", "dp"), None, "tensor", None),
        P(("groups", "dp"), None),
        P(("groups", "dp")),
        P(None, "groups"),
        P("groups", "tensor", None),
        P("tensor", "dp"),
        P(None, ("groups", "tensor"), "dp"),
    )
    out_specs = P(None, ("groups", "tensor"), "dp")
    return jax.shard_map(local, mesh=mesh, in_specs=in_specs, out_specs=out_specs, check_vma=False)
```

profile of v0, /device:TPU:0, one launch (start us, length us, event | category | flops | bytes accessed | tf_op | source)
XLA Modules:
  0.0 192.5 jit_solution(11708064764896520419)
XLA Ops:
  6.5 0.8 fusion.90
  7.4 1.6 fusion.77
  11.4 0.9 copy.56
  12.2 2.7 %fusion.87 = (bf16[2048,2,128]{2,1,0:T(2,128)(2,1)S(1)}, bf16[2048,2,128]{2,1,0:T(2,128)(2,1)S(1)}) fusion(bf16[2048,2,256]{2,1,0:T(2,128)(2,1)} %param.15), kind=kLoop, calls=%fused_computation.195 | loop fusion | bytes 4194304 | tf_op jit(solution)/shard_map/slice | solution.py:40
  15.9 0.6 fusion.23
  16.8 0.6 gather_fusion.1
  18.0 14.8 %all_gather.28 = bf16[4,8,2,256]{3,1,2,0:T(8,128)(2,1)S(1)} all-gather(bf16[1,8,2,256]{3,1,2,0:T(8,128)(2,1)S(1)} %copy.62), channel_id=1, replica_groups=mesh['groups'=2,'dp'=4,'tensor'=4] {'dp'}, dimensions={0}, use_global_device_ids=true | all-gather | bytes 40960 | tf_op jit(solution)/shard_map/all_gather | solution.py:64
  32.9 0.7 dynamic-slice_convert_fusion.3
  34.2 0.6 dynamic-slice.4
  34.8 1.3 dynamic-update-slice
  36.8 11.7 %all-reduce = bf16[4]{0:T(256)(128)(2,1)S(1)} all-reduce(bf16[4]{0:T(256)(128)(2,1)S(1)} %dynamic-update-slice), channel_id=1, replica_groups=mesh['groups'=2,'dp'=4,'tensor'=4] {'dp'}, use_global_device_ids=true, to_apply=%add | all-reduce | flops 4 | bytes 16
  49.1 0.6 gather_fusion
  50.7 13.1 %all_gather.30 = bf16[4,8,2,256]{3,1,2,0:T(8,128)(2,1)S(1)} all-gather(bf16[1,8,2,256]{3,1,2,0:T(8,128)(2,1)S(1)} %constant_dynamic-slice_fusion.4), channel_id=1, replica_groups=mesh['groups'=2,'dp'=4,'tensor'=4] {'dp'}, dimensions={0}, use_global_device_ids=true | all-gather | bytes 40960 | tf_op jit(solution)/shard_map/all_gather | solution.py:64
  63.9 0.6 dynamic-slice_convert_fusion.2
  65.2 1.3 dynamic-update-slice.1
  67.1 8.4 %all-reduce.1 = bf16[4]{0:T(256)(128)(2,1)S(1)} all-reduce(bf16[4]{0:T(256)(128)(2,1)S(1)} %dynamic-update-slice.1), channel_id=1, replica_groups=mesh['groups'=2,'dp'=4,'tensor'=4] {'dp'}, use_global_device_ids=true, to_apply=%add.1 | all-reduce | flops 4 | bytes 16
  76.1 0.6 gather_fusion.3
  77.7 13.1 %all_gather.32 = bf16[4,8,2,256]{3,1,2,0:T(8,128)(2,1)S(1)} all-gather(bf16[1,8,2,256]{3,1,2,0:T(8,128)(2,1)S(1)} %constant_dynamic-slice_fusion.2), channel_id=1, replica_groups=mesh['groups'=2,'dp'=4,'tensor'=4] {'dp'}, dimensions={0}, use_global_device_ids=true | all-gather | bytes 40960 | tf_op jit(solution)/shard_map/all_gather | solution.py:64
  90.9 0.7 dynamic-slice_convert_fusion.1
  91.5 1.4 dynamic-update-slice.2
  93.0 10.5 %all-reduce.2 = bf16[4]{0:T(256)(128)(2,1)S(1)} all-reduce(bf16[4]{0:T(256)(128)(2,1)S(1)} %dynamic-update-slice.2), channel_id=1, replica_groups=mesh['groups'=2,'dp'=4,'tensor'=4] {'dp'}, use_global_device_ids=true, to_apply=%add.2 | all-reduce | flops 4 | bytes 16
  104.0 0.6 gather_fusion.5
  105.6 13.1 %all_gather.34 = bf16[4,8,2,256]{3,1,2,0:T(8,128)(2,1)S(1)} all-gather(bf16[1,8,2,256]{3,1,2,0:T(8,128)(2,1)S(1)} %constant_dynamic-slice_fusion), channel_id=1, replica_groups=mesh['groups'=2,'dp'=4,'tensor'=4] {'dp'}, dimensions={0}, use_global_device_ids=true | all-gather | bytes 40960 | tf_op jit(solution)/shard_map/all_gather | solution.py:64
  118.8 0.6 dynamic-slice_convert_fusion
  119.4 1.3 dynamic-update-slice.3
  120.7 8.4 %all-reduce.3 = bf16[4]{0:T(256)(128)(2,1)S(1)} all-reduce(bf16[4]{0:T(256)(128)(2,1)S(1)} %dynamic-update-slice.3), channel_id=1, replica_groups=mesh['groups'=2,'dp'=4,'tensor'=4] {'dp'}, use_global_device_ids=true, to_apply=%add.3 | all-reduce | flops 4 | bytes 16
  129.7 0.6 gather_fusion.7
  132.5 13.8 %all_gather.35 = bf16[4,16,2048]{2,0,1:T(4,128)(2,1)S(1)} all-gather(bf16[4,4,2048]{2,0,1:T(4,128)(2,1)S(1)} %pad_maximum_fusion), channel_id=1, replica_groups=mesh['groups'=2,'dp'=4,'tensor'=4] {'dp'}, dimensions={1}, use_global_device_ids=true | all-gather | bytes 327680 | tf_op jit(solution)/shard_map/all_gather | solution.py:108
  146.3 5.8 %fusion.2 = bf16[4,16,2048]{2,1,0:T(8,128)(2,1)} fusion(bf16[2048,2048]{1,0:T(8,128)(2,1)} %param.16, bf16[4,16,2048]{2,0,1:T(4,128)(2,1)S(1)} %all_gather.35), kind=kOutput, calls=%fused_computation.12 | convolution fusion | flops 537001984 | bytes 8912896 | tf_op jit(solution)/shard_map/snf,fc->snc/dot_general | solution.py:106
  152.2 0.6 dynamic-slice.8
  153.4 30.6 %all-reduce.7.cloned.1.call-done = bf16[4,16,2048]{2,1,0:T(8,128)(2,1)} async-done(((bf16[4,16,2048]{2,1,0:T(8,128)(2,1)}), bf16[4,16,2048]{2,1,0:T(8,128)(2,1)}) %all-reduce.7.cloned.1.call-update) | async-done | bytes 262160
  184.1 1.6 add_convert_fusion
  (86 shorter events, 6.8 us)
Async XLA Ops:
  6.5 10.2 %copy-start = (bf16[8,4,2,256]{3,2,1,0:T(2,128)(2,1)S(1)}, bf16[8,4,2,256]{3,2,1,0:T(2,128)(2,1)}, u32[]{:S(2)}) copy-start(bf16[8,4,2,256]{3,2,1,0:T(2,128)(2,1)} %param.11) | copy-start | bytes 98308
  6.5 177.5 %all-reduce.7.cloned.1.call-start = ((), (), s32[]{:S(2)}) async-start(), calls=%async_computation | async-start | bytes 524288
  15.9 0.7 copy-start.4
  15.9 17.0 %copy-start.5 = (s32[4]{0:T(128)S(1)}, s32[4]{0:T(128)}, u32[]{:S(2)}) copy-start(s32[4]{0:T(128)} %param.13) | copy-start | bytes 52
  15.9 18.3 %copy-start.7 = (u32[32]{0:T(128)S(1)}, u32[32]{0:T(128)}, u32[]{:S(2)}) copy-start(u32[32]{0:T(128)} %constant.76) | copy-start | bytes 388
  15.9 34.0 %copy-start.3 = (bf16[4,4,2,256]{3,2,1,0:T(2,128)(2,1)S(1)}, bf16[4,4,2,256]{3,2,1,0:T(2,128)(2,1)}, u32[]{:S(2)}) copy-start(bf16[4,4,2,256]{3,2,1,0:T(2,128)(2,1)} %param.10) | copy-start | bytes 49156
  16.6 114.0 %copy-start.2 = (bf16[4,4,16,128]{3,2,1,0:T(8,128)(2,1)S(1)}, bf16[4,4,16,128]{3,2,1,0:T(8,128)(2,1)}, u32[]{:S(2)}) copy-start(bf16[4,4,16,128]{3,2,1,0:T(8,128)(2,1)} %param.9) | copy-start | bytes 196612
  146.3 5.9 %copy-start.6 = (u32[32]{0:T(128)S(1)}, u32[32]{0:T(128)}, u32[]{:S(2)}) copy-start(u32[32]{0:T(128)} %constant.100) | copy-start | bytes 388
  146.3 37.8 %copy-start.1 = (bf16[4,4,2048]{2,1,0:T(4,128)(2,1)S(1)}, bf16[4,4,2048]{2,1,0:T(4,128)(2,1)}, u32[]{:S(2)}) copy-start(bf16[4,4,2048]{2,1,0:T(4,128)(2,1)} %param.17) | copy-start | bytes 196612
Sparse Core Ops, SparseCore 0:
  152.3 31.7 all-reduce.6
where the time goes:
time: 193 us; the launch traced here: 192 us
  blocking collectives  107 us (55%)
  waiting for transfers between devices  30.6 us (16%)
  between operations  22 us (11%)
  local copies, waits for them, and re-layouts  16.8 us (9%)
  matrix products  8.33 us (4%)
  other arithmetic  7.8 us (4%)
    all_gather x4, blocking collectives, local(): lax.all_gather(export_tail, 'dp', axis=0, tiled=True)  54.2 us
    unnamed x4, blocking collectives  39 us
    unnamed x2, waiting for transfers between devices  30.6 us
    all_gather x1, blocking collectives, local(): lax.all_gather(head_outputs, 'dp', axis=1, tiled=True)  13.8 us
    unnamed x27, local copies, waits for them, and re-layouts  6.63 us
    dot_general x1, matrix products, local(): jnp.einsum('snf,fc->snc', lax.all_gather(head_outputs, 'dp', axis=1, tile...  5.85 us
  transfers between devices with their start and end apart: 1, of which 1 were waited for; matrix products, arithmetic and copies ran while one was open for 0% of the time, Pallas kernels for 0%

commit v1 on v0

v1 whole, which is shorter than its diff:
```python
import functools
import math

import jax
import jax.numpy as jnp
from jax import lax
from jax.experimental import pallas as pl
from jax.experimental.pallas import tpu as pltpu
from jax.sharding import PartitionSpec as P

MESH = pl.DeviceIdType.MESH
BLOCK = 128


def kernel(
    dims, q_ref, keys_ref, values_ref, pack_ref, fork_ref, weight_ref, residual_ref, out_ref,
    q_flat, scores, tail_scores, packs, weight, heads, partial, landed,
    weight_sem, own_sem, pack_send, pack_recv, head_send, head_recv, part_send, part_recv,
):
    dp, tensor, steps, nodes, head_count, kv_local, head_dim, pages, page, tile = dims
    pairs = steps * nodes
    rows = pairs * head_count
    group = head_count // kv_local
    pool_rows = pages * page * kv_local
    new_rows = pairs * kv_local
    me = lax.axis_index("dp")
    me_tensor = lax.axis_index("tensor")
    factor = head_dim ** (-0.5) * math.log2(math.e)

    weight_copy = pltpu.make_async_copy(weight_ref, weight, weight_sem)
    weight_copy.start()
    own_copy = pltpu.make_async_copy(pack_ref, packs.at[me], own_sem)
    own_copy.start()

    barrier = pltpu.get_barrier_semaphore()
    for hop in range(1, dp):
        pl.semaphore_signal(
            barrier, inc=1, device_id={"dp": lax.rem(me + hop, dp)}, device_id_type=MESH
        )
    for hop in range(1, tensor):
        pl.semaphore_signal(
            barrier, inc=1, device_id={"tensor": lax.rem(me_tensor + hop, tensor)},
            device_id_type=MESH,
        )
    pl.semaphore_wait(barrier, dp + tensor - 2)

    pack_copies = []
    for hop in range(1, dp):
        copy = pltpu.make_async_remote_copy(
            src_ref=pack_ref,
            dst_ref=packs.at[me],
            send_sem=pack_send.at[hop],
            recv_sem=pack_recv.at[hop],
            device_id={"dp": lax.rem(me + hop, dp)},
            device_id_type=MESH,
        )
        copy.start()
        pack_copies.append(copy)

    q_flat[...] = q_ref[...].astype(jnp.float32)
    q = jnp.concatenate(
        [q_flat[pl.ds(h, pairs, stride=head_count), :] for h in range(head_count)], axis=0
    ).astype(jnp.bfloat16)
    contract = (((1,), (1,)), ((), ()))

    width = scores.shape[2]
    chunks = scores.shape[0]
    row_kv = lax.broadcasted_iota(jnp.int32, (rows, width), 0) // (group * pairs)
    col_kv = lax.broadcasted_iota(jnp.int32, (rows, width), 1) % kv_local
    same = row_kv == col_kv

    def score_chunk(c, highest):
        start = pl.multiple_of(c * width, width)
        s = lax.dot_general(
            q, keys_ref[pl.ds(start, width), :], contract, preferred_element_type=jnp.float32
        )
        s = jnp.where(same, s, -jnp.inf)
        scores[c] = s
        return jnp.maximum(highest, s.max(-1, keepdims=True))

    prompt_max = lax.fori_loop(
        0, chunks, score_chunk, jnp.full((rows, 1), -jnp.inf, jnp.float32)
    )

    def weigh_chunk(c, carry):
        total, acc = carry
        start = pl.multiple_of(c * width, width)
        w = jnp.exp2((scores[c] - prompt_max) * factor)
        total = total + w.sum(-1, keepdims=True)
        acc = acc + jnp.dot(
            w.astype(jnp.bfloat16), values_ref[pl.ds(start, width), :],
            preferred_element_type=jnp.float32,
        )
        return total, acc

    prompt_sum, prompt_acc = lax.fori_loop(
        0, chunks, weigh_chunk,
        (jnp.zeros((rows, 1), jnp.float32), jnp.zeros((rows, head_dim), jnp.float32)),
    )

    forks = fork_ref[...].astype(jnp.float32)
    total_nodes = forks.shape[1]
    ids = lax.broadcasted_iota(jnp.int32, (pairs, total_nodes), 1).astype(jnp.float32)
    pair_at = lax.broadcasted_iota(jnp.int32, (pairs, 1), 0)
    pair_step = pair_at // nodes
    current = (pair_at % nodes + me * nodes).astype(jnp.float32)
    places = [None] * steps
    for step in reversed(range(steps)):
        reached = pair_step >= step
        places[step] = jnp.where(reached, current, -1.0)
        parent = forks[step : step + 1, :]
        parent = jnp.where(parent >= 0.0, parent, ids)
        found = jnp.where(ids == current, parent, 0.0).sum(-1, keepdims=True)
        current = jnp.where(reached, found, current)
    lane = lax.broadcasted_iota(jnp.int32, (pairs, BLOCK), 1)
    wanted = jnp.broadcast_to(current, (pairs, BLOCK))
    for step in range(steps):
        wanted = jnp.where(
            lane >= pool_rows + step * nodes * kv_local, places[step], wanted
        )
    is_new = lane >= pool_rows
    new_node = ((lane - pool_rows) // kv_local % nodes).astype(jnp.float32)
    inside = lane < pool_rows + new_rows
    parity = lane % kv_local

    own_copy.wait()
    for copy in pack_copies:
        copy.wait()

    def tail_score(d, highest):
        s = lax.dot_general(
            q, packs[d, :BLOCK, :], contract, preferred_element_type=jnp.float32
        )
        node = packs[d, pool_rows + new_rows : pool_rows + new_rows + 16, :].astype(jnp.float32)
        node = jnp.where(is_new, new_node, jnp.broadcast_to(node[0:1, :], (pairs, BLOCK)))
        base = (d * nodes).astype(jnp.float32)
        seen = inside & (node >= 0.0) & (node + base == wanted)
        pieces = []
        for k in range(kv_local):
            keep = (seen & (parity == k))[None]
            part = s[k * group * pairs : (k + 1) * group * pairs].reshape(group, pairs, BLOCK)
            pieces.append(jnp.where(keep, part, -jnp.inf).reshape(group * pairs, BLOCK))
        s = jnp.concatenate(pieces, axis=0)
        tail_scores[d] = s
        return jnp.maximum(highest, s.max(-1, keepdims=True))

    highest = lax.fori_loop(0, dp, tail_score, prompt_max)
    carried = jnp.exp2((prompt_max - highest) * factor)

    def tail_weigh(d, carry):
        total, acc = carry
        w = jnp.exp2((tail_scores[d] - highest) * factor)
        total = total + w.sum(-1, keepdims=True)
        acc = acc + jnp.dot(
            w.astype(jnp.bfloat16), packs[d, BLOCK : 2 * BLOCK, :],
            preferred_element_type=jnp.float32,
        )
        return total, acc

    denominator, mixed = lax.fori_loop(
        0, dp, tail_weigh, (prompt_sum * carried, prompt_acc * carried)
    )
    attended = (mixed / denominator).astype(jnp.bfloat16)
    for h in range(head_count):
        heads[me, :, h * head_dim : (h + 1) * head_dim] = attended[h * pairs : (h + 1) * pairs]

    head_copies = []
    for hop in range(1, dp):
        copy = pltpu.make_async_remote_copy(
            src_ref=heads.at[me],
            dst_ref=heads.at[me],
            send_sem=head_send.at[hop],
            recv_sem=head_recv.at[hop],
            device_id={"dp": lax.rem(me + hop, dp)},
            device_id_type=MESH,
        )
        copy.start()
        head_copies.append(copy)
    weight_copy.wait()
    for copy in head_copies:
        copy.wait()

    columns = weight.shape[1]
    per_tensor = dp // tensor
    gathered = heads[...].reshape(dp * pairs, head_count * head_dim)
    part_copies = []
    for at in range(columns // tile):
        here = slice(at * tile, (at + 1) * tile)
        product = jnp.dot(gathered, weight[:, here], preferred_element_type=jnp.float32)
        partial[at] = product.astype(jnp.bfloat16).reshape(tensor, per_tensor * pairs, tile)
        for hop in range(1, tensor):
            peer = lax.rem(me_tensor + hop, tensor)
            copy = pltpu.make_async_remote_copy(
                src_ref=partial.at[at, peer],
                dst_ref=landed.at[at, hop],
                send_sem=part_send.at[at, hop],
                recv_sem=part_recv.at[at, hop],
                device_id={"tensor": peer},
                device_id_type=MESH,
            )
            copy.start()
            part_copies.append(copy)
    for at in range(columns // tile):
        here = slice(at * tile, (at + 1) * tile)
        for copy in part_copies[at * (tensor - 1) : (at + 1) * (tensor - 1)]:
            copy.wait()
        total = partial[at, me_tensor].astype(jnp.float32)
        for hop in range(1, tensor):
            total = total + landed[at, hop].astype(jnp.float32)
        out_ref[:, here] = (residual_ref[:, here].astype(jnp.float32) + total).astype(jnp.bfloat16)


def local(
    dp, tensor,
    query, new_kv, tail_pool, page_table, tail_len, fork_parent, prompt_kv, out_weight, residual,
):
    steps, nodes, head_count, head_dim = query.shape
    pages, page, kv_local, _ = tail_pool.shape
    prompt = prompt_kv.shape[0]
    columns = out_weight.shape[1]
    pairs = steps * nodes
    rows = pairs * head_count
    per_tensor = dp // tensor
    pool_rows = pages * page * kv_local
    new_rows = pairs * kv_local
    tile = min(512, columns)
    width = 1024
    chunks = prompt * kv_local // width
    bf16 = jnp.bfloat16

    keys = prompt_kv[..., :head_dim].reshape(prompt * kv_local, head_dim)
    values = prompt_kv[..., head_dim:].reshape(prompt * kv_local, head_dim)

    at_page = jnp.arange(pages, dtype=jnp.int32)
    match = page_table[:, :, None] == at_page
    table_node = jnp.arange(nodes, dtype=jnp.int32)[:, None, None]
    logical = jnp.arange(page_table.shape[1], dtype=jnp.int32)[None, :, None]
    owner = jnp.where(match, table_node, 0).sum((0, 1))
    filled = jnp.where(match, tail_len[:, None, None] - logical * page, 0).sum((0, 1))
    live = jnp.arange(page, dtype=jnp.int32)[None, :] < filled[:, None]
    node_row = jnp.where(live, owner[:, None], -1).astype(bf16)
    node_row = jnp.repeat(node_row.reshape(-1), kv_local)
    meta = jnp.broadcast_to(jnp.pad(node_row, (0, head_dim - pool_rows)), (16, head_dim))
    spare = BLOCK - pool_rows - new_rows
    pack = jnp.concatenate(
        [
            tail_pool[..., :head_dim].reshape(pool_rows, head_dim),
            new_kv[..., :head_dim].reshape(new_rows, head_dim),
            meta,
            jnp.zeros((spare - 16, head_dim), bf16),
            tail_pool[..., head_dim:].reshape(pool_rows, head_dim),
            new_kv[..., head_dim:].reshape(new_rows, head_dim),
            jnp.zeros((spare, head_dim), bf16),
        ]
    )
    residual_rows = (
        residual.reshape(steps, per_tensor, nodes, columns)
        .transpose(1, 0, 2, 3)
        .reshape(per_tensor * pairs, columns)
    )

    dims = (dp, tensor, steps, nodes, head_count, kv_local, head_dim, pages, page, tile)
    vmem = pl.BlockSpec(memory_space=pltpu.VMEM)
    tiles = columns // tile
    dma = pltpu.SemaphoreType.DMA
    out = pl.pallas_call(
        functools.partial(kernel, dims),
        out_shape=jax.ShapeDtypeStruct((per_tensor * pairs, columns), bf16),
        in_specs=[vmem] * 5 + [pl.BlockSpec(memory_space=pl.ANY), vmem],
        out_specs=vmem,
        scratch_shapes=[
            pltpu.VMEM((rows, head_dim), jnp.float32),
            pltpu.VMEM((chunks, rows, width), jnp.float32),
            pltpu.VMEM((dp, rows, BLOCK), jnp.float32),
            pltpu.VMEM((dp, 2 * BLOCK, head_dim), bf16),
            pltpu.VMEM(out_weight.shape, bf16),
            pltpu.VMEM((dp, pairs, head_count * head_dim), bf16),
            pltpu.VMEM((tiles, tensor, per_tensor * pairs, tile), bf16),
            pltpu.VMEM((tiles, tensor, per_tensor * pairs, tile), bf16),
            dma,
            dma,
            dma((dp,)),
            dma((dp,)),
            dma((dp,)),
            dma((dp,)),
            dma((tiles, tensor)),
            dma((tiles, tensor)),
        ],
        compiler_params=pltpu.CompilerParams(
            collective_id=0, has_side_effects=True, vmem_limit_bytes=48 * 1024 * 1024
        ),
    )(
        query.reshape(rows, head_dim), keys, values, pack, fork_parent, out_weight, residual_rows
    )
    return (
        out.reshape(per_tensor, steps, nodes, columns)
        .transpose(1, 0, 2, 3)
        .reshape(residual.shape)
    )


def solution(mesh):
    in_specs = (
        P(None, ("groups", "dp"), "tensor", None),
        P(None, ("groups", "dp"), "tensor", None),
        P(("groups", "dp"), None, "tensor", None),
        P(("groups", "dp"), None),
        P(("groups", "dp")),
        P(None, "groups"),
        P("groups", "tensor", None),
        P("tensor", "dp"),
        P(None, ("groups", "tensor"), "dp"),
    )
    out_specs = P(None, ("groups", "tensor"), "dp")
    body = functools.partial(local, mesh.shape["dp"], mesh.shape["tensor"])
    return jax.shard_map(body, mesh=mesh, in_specs=in_specs, out_specs=out_specs, check_vma=False)
```

time: 193 us -> 31.9 us (0.17)
  blocking collectives: 107 us -> 0 us
  waiting for transfers between devices: 30.6 us -> 0 us
  Pallas kernels: 0 us -> 23.9 us
  between operations: 22 us -> 0.09 us
  local copies, waits for them, and re-layouts: 16.8 us -> 6.09 us
  matrix products: 8.33 us -> 0 us
  other arithmetic: 7.8 us -> 1.57 us
    all_gather x5 -> x0, blocking collectives: 68 us -> none  [the longest x4 54.2 us: local(): lax.all_gather(export_tail, 'dp', axis=0, tiled=True)]
    unnamed x4 -> x0, blocking collectives: 39 us -> none
    unnamed x2 -> x0, waiting for transfers between devices: 30.6 us -> none
    pallas_call x0 -> x1, Pallas kernels: none -> 23.9 us  [local(): pl.pallas_call(functools.partial(kernel, dims), out_shape=jax.ShapeDtypeS...]
    dot_general x11 -> x0, matrix products: 8.33 us -> none  [the longest x1 5.85 us: local(): jnp.einsum('snf,fc->snc', lax.all_gather(head_outputs, 'dp', axis=1, tile...]
    unnamed x27 -> x10, local copies, waits for them, and re-layouts: 6.63 us -> 0.06 us
    gather x9 -> x0, local copies, waits for them, and re-layouts: 5.37 us -> none  [the longest x4 2.57 us: local(): fetched_lengths = got_lengths[source_device].astype(jnp.int32)]
    convert_element_type x5 -> x1, other arithmetic: 4.12 us -> 0.08 us  [local(): node_row = jnp.where(live, owner[:, None], -1).astype(bf16)]
  transfers between devices with their start and end apart: 1 -> 0, of which waited for: 1 -> 0; matrix products, arithmetic and copies ran while one was open for 0% -> 0% of each run, Pallas kernels for 0% -> 0%
where the time goes in v1:
time: 31.9 us; the launch traced here: 31.6 us
  Pallas kernels  23.9 us (75%)
  local copies, waits for them, and re-layouts  6.09 us (19%)
  other arithmetic  1.57 us (5%)
    pallas_call x1, Pallas kernels, local(): pl.pallas_call(functools.partial(kernel, dims), out_shape=jax.ShapeDtypeS...  23.9 us
    slice x1, local copies, waits for them, and re-layouts, local(): values = prompt_kv[..., head_dim:].reshape(prompt * kv_local, head_dim)  2.71 us
    another operation x1, local copies, waits for them, and re-layouts, local(): residual_rows = residual.reshape(steps, per_tensor, nodes, columns).trans...  0.86 us
    reduce_sum x1, other arithmetic, local(): jnp.where(match, tail_len[:, None, None] - logical * page, 0).sum((0, 1))  0.77 us
    slice x1, local copies, waits for them, and re-layouts, local(): tail_pool[..., head_dim:].reshape(pool_rows, head_dim)  0.76 us
    slice x1, local copies, waits for them, and re-layouts, local(): new_kv[..., head_dim:].reshape(new_rows, head_dim)  0.73 us
    sub x1, other arithmetic, local(): tail_len[:, None, None] - logical * page  0.72 us
    another operation x1, local copies, waits for them, and re-layouts, local(): return out.reshape(per_tensor, steps, nodes, columns).transpose(1, 0, 2,...  0.66 us

profile of v1, /device:TPU:0, one launch (start us, length us, event | category | flops | bytes accessed | tf_op | source)
XLA Modules:
  0.0 31.6 jit_solution(3549482185376155197)
XLA Ops:
  0.0 0.7 %broadcast_subtract_fusion = s32[4,2]{0,1:T(2,128)S(1)} fusion(s32[4]{0:T(128)} %param.13, s32[2]{0:T(128)S(1)} %iota_multiply_fusion), kind=kLoop, calls=%fused_computation.13 | loop fusion | flops 8 | bytes 56 | tf_op jit(solution)/shard_map/sub | solution.py:239
  0.7 0.8 %select_reduce_fusion.1 = (s32[8]{0:T(128)S(1)}, s32[8]{0:T(128)S(1)}) fusion(s32[4,2]{0,1:T(2,128)S(1)} %broadcast_subtract_fusion, s32[4,2]{0,1:T(2,128)} %param.12), kind=kLoop, calls=%fused_computation.9 | loop fusion | flops 304 | bytes 128 | tf_op jit(solution)/shard_map/reduce_sum | solution.py:239
  1.5 0.1 select_convert_fusion
  1.6 0.1 convert_element_type.10
  1.7 0.1 broadcast_in_dim.59
  1.7 0.1 reshape.78
  1.9 0.7 %fusion.2 = (bf16[4,4,2,128]{3,2,1,0:T(2,128)(2,1)S(1)}, bf16[4,4,2,128]{3,2,1,0:T(2,128)(2,1)S(1)}) fusion(bf16[4,4,2,256]{3,2,1,0:T(2,128)(2,1)} %param.10), kind=kLoop, calls=%fused_computation.16 | loop fusion | bytes 32768 | tf_op jit(solution)/shard_map/slice | solution.py:252
  2.6 0.8 %fusion.1 = (bf16[8,4,2,128]{3,2,1,0:T(2,128)(2,1)S(1)}, bf16[8,4,2,128]{3,2,1,0:T(2,128)(2,1)S(1)}) fusion(bf16[8,4,2,256]{3,2,1,0:T(2,128)(2,1)} %param.11), kind=kLoop, calls=%fused_computation.15 | loop fusion | bytes 65536 | tf_op jit(solution)/shard_map/slice | solution.py:251
  3.5 0.9 %reshape_transpose_reshape.6.residual_ref = bf16[16,2048]{1,0:T(8,128)(2,1)S(1)} reshape(bf16[4,4,2048]{2,1,0:T(4,128)(2,1)} %param.17) | data formatting | bytes 131072 | tf_op jit(solution)/shard_map/reshape;transpose;reshape | solution.py:259
  4.3 0.0 copy-start
  4.3 0.0 copy-start.1
  4.3 2.7 %fusion = (bf16[2048,2,128]{2,1,0:T(2,128)(2,1)S(1)}, bf16[2048,2,128]{2,1,0:T(2,128)(2,1)S(1)}) fusion(bf16[2048,2,256]{2,1,0:T(2,128)(2,1)} %param.15), kind=kLoop, calls=%fused_computation.14 | loop fusion | bytes 4194304 | tf_op jit(solution)/shard_map/slice | solution.py:232
  7.1 0.0 copy-done
  7.1 0.0 copy-done.1
  7.1 23.9 %shard_map.91 = bf16[16,2048]{1,0:T(8,128)(2,1)S(1)} custom-call(bf16[256,128]{1,0:T(8,128)(2,1)S(1)} %bitcast.9, bf16[4096,128]{1,0:T(8,128)(2,1)S(1)} %bitcast.8, bf16[4096,128]{1,0:T(8,128)(2,1)S(1)} %bitcast.7, bf16[256,128]{1,0:T(8,128)(2,1)S(1)} %constant_dynamic-update-slice_fusion.pack_ref, s32[4,16]{1,0:T(4,128)S(1)} %copy-done.1, ...), custom_call_target="tpu_custom_call" | custom-call | tf_op jit(solution)/shard_map/pallas_call | solution.py:266
  31.0 0.7 %reshape_transpose_reshape.7 = bf16[4,4,2048]{2,1,0:T(4,128)(2,1)} reshape(bf16[16,2048]{1,0:T(8,128)(2,1)S(1)} %shard_map.91) | data formatting | bytes 131072 | tf_op jit(solution)/shard_map/reshape;transpose;reshape | solution.py:298
  (9 shorter events, 0.1 us)
Async XLA Ops:
  4.3 2.7 %copy-start = (bf16[4,4,16,128]{3,2,1,0:T(8,128)(2,1)S(1)}, bf16[4,4,16,128]{3,2,1,0:T(8,128)(2,1)}, u32[]{:S(2)}) copy-start(bf16[4,4,16,128]{3,2,1,0:T(8,128)(2,1)} %param.9) | copy-start | bytes 196612
  4.3 2.7 %copy-start.1 = (s32[4,16]{1,0:T(4,128)S(1)}, s32[4,16]{1,0:T(4,128)}, u32[]{:S(2)}) copy-start(s32[4,16]{1,0:T(4,128)} %fork_ref.1) | copy-start | bytes 772

commit v2 on v1

--- a/solution.py
+++ b/solution.py
@@ -13,9 +13,12 @@
 
 
 def kernel(
-    dims, q_ref, keys_ref, values_ref, pack_ref, fork_ref, weight_ref, residual_ref, out_ref,
-    q_flat, scores, tail_scores, packs, weight, heads, partial, landed,
-    weight_sem, own_sem, pack_send, pack_recv, head_send, head_recv, part_send, part_recv,
+    dims, table_ref, len_ref, q_ref, fork_ref, residual_ref, prompt_ref, pool_ref, new_ref,
+    weight_ref, out_ref,
+    q_flat, prompt_keys, prompt_values, scores, tail_scores, packs, owners, weight, heads,
+    partial, landed,
+    weight_sem, own_sem, prompt_sem, pack_send, pack_recv, owner_send, owner_recv,
+    head_send, head_recv, part_send, part_recv,
 ):
     dp, tensor, steps, nodes, head_count, kv_local, head_dim, pages, page, tile = dims
     pairs = steps * nodes
@@ -27,10 +30,42 @@
     me_tensor = lax.axis_index("tensor")
     factor = head_dim ** (-0.5) * math.log2(math.e)
 
+    total_chunks, chunk_prompt = prompt_keys.shape[0], prompt_keys.shape[1]
+    pool_tokens = pages * page
+    half = BLOCK // kv_local
+
+    own_copies = []
+    for part in range(2):
+        lanes = slice(part * head_dim, (part + 1) * head_dim)
+        own_copies.append(
+            pltpu.make_async_copy(
+                pool_ref.at[:, :, lanes], packs.at[me, part, 0:pool_tokens], own_sem.at[part, 0]
+            )
+        )
+        own_copies.append(
+            pltpu.make_async_copy(
+                new_ref.at[:, :, lanes], packs.at[me, part, pool_tokens : pool_tokens + pairs],
+                own_sem.at[part, 1],
+            )
+        )
+    for copy in own_copies:
+        copy.start()
+
+    def prompt_copy(c, part):
+        return pltpu.make_async_copy(
+            prompt_ref.at[
+                pl.ds(c * chunk_prompt, chunk_prompt), :,
+                part * head_dim : (part + 1) * head_dim,
+            ],
+            (prompt_values if part else prompt_keys).at[c],
+            prompt_sem.at[part, c],
+        )
+
+    for part in range(2):
+        for c in range(total_chunks):
+            prompt_copy(c, part).start()
     weight_copy = pltpu.make_async_copy(weight_ref, weight, weight_sem)
     weight_copy.start()
-    own_copy = pltpu.make_async_copy(pack_ref, packs.at[me], own_sem)
-    own_copy.start()
 
     barrier = pltpu.get_barrier_semaphore()
     for hop in range(1, dp):
@@ -42,20 +77,38 @@
             barrier, inc=1, device_id={"tensor": lax.rem(me_tensor + hop, tensor)},
             device_id_type=MESH,
         )
+
+    spot = lax.broadcasted_iota(jnp.int32, (16, BLOCK), 1) // kv_local
+    owner = jnp.full((16, BLOCK), -1.0, jnp.float32)
+    for n in range(nodes):
+        for j in range(pages // nodes):
+            held = (spot // page == table_ref[j, n]) & (spot % page + j * page < len_ref[n])
+            owner = jnp.where(held & (spot < pool_tokens), float(n), owner)
+    owners[me] = owner.astype(jnp.bfloat16)
+    used = pool_tokens + pairs
+    for part in range(2):
+        packs[me, part, used:half] = jnp.zeros(
+            (half - used, kv_local, head_dim), jnp.bfloat16
+        )
+    for copy in own_copies:
+        copy.wait()
     pl.semaphore_wait(barrier, dp + tensor - 2)
 
     pack_copies = []
     for hop in range(1, dp):
-        copy = pltpu.make_async_remote_copy(
-            src_ref=pack_ref,
-            dst_ref=packs.at[me],
-            send_sem=pack_send.at[hop],
-            recv_sem=pack_recv.at[hop],
-            device_id={"dp": lax.rem(me + hop, dp)},
-            device_id_type=MESH,
-        )
-        copy.start()
-        pack_copies.append(copy)
+        for buffer, send, recv in (
+            (packs, pack_send, pack_recv), (owners, owner_send, owner_recv)
+        ):
+            copy = pltpu.make_async_remote_copy(
+                src_ref=buffer.at[me],
+                dst_ref=buffer.at[me],
+                send_sem=send.at[hop],
+                recv_sem=recv.at[hop],
+                device_id={"dp": lax.rem(me + hop, dp)},
+                device_id_type=MESH,
+            )
+            copy.start()
+            pack_copies.append(copy)
 
     q_flat[...] = q_ref[...].astype(jnp.float32)
     q = jnp.concatenate(
@@ -70,9 +123,9 @@
     same = row_kv == col_kv
 
     def score_chunk(c, highest):
-        start = pl.multiple_of(c * width, width)
+        prompt_copy(c, 0).wait()
         s = lax.dot_general(
-            q, keys_ref[pl.ds(start, width), :], contract, preferred_element_type=jnp.float32
+            q, prompt_keys.at[c].reshape(width, head_dim)[...], contract, preferred_element_type=jnp.float32
         )
         s = jnp.where(same, s, -jnp.inf)
         scores[c] = s
@@ -84,11 +137,11 @@
 
     def weigh_chunk(c, carry):
         total, acc = carry
-        start = pl.multiple_of(c * width, width)
+        prompt_copy(c, 1).wait()
         w = jnp.exp2((scores[c] - prompt_max) * factor)
         total = total + w.sum(-1, keepdims=True)
         acc = acc + jnp.dot(
-            w.astype(jnp.bfloat16), values_ref[pl.ds(start, width), :],
+            w.astype(jnp.bfloat16), prompt_values.at[c].reshape(width, head_dim)[...],
             preferred_element_type=jnp.float32,
         )
         return total, acc
@@ -123,15 +176,14 @@
     inside = lane < pool_rows + new_rows
     parity = lane % kv_local
 
-    own_copy.wait()
     for copy in pack_copies:
         copy.wait()
 
     def tail_score(d, highest):
         s = lax.dot_general(
-            q, packs[d, :BLOCK, :], contract, preferred_element_type=jnp.float32
-        )
-        node = packs[d, pool_rows + new_rows : pool_rows + new_rows + 16, :].astype(jnp.float32)
+            q, packs.at[d, 0].reshape(BLOCK, head_dim)[...], contract, preferred_element_type=jnp.float32
+        )
+        node = owners[d].astype(jnp.float32)
         node = jnp.where(is_new, new_node, jnp.broadcast_to(node[0:1, :], (pairs, BLOCK)))
         base = (d * nodes).astype(jnp.float32)
         seen = inside & (node >= 0.0) & (node + base == wanted)
@@ -152,7 +204,7 @@
         w = jnp.exp2((tail_scores[d] - highest) * factor)
         total = total + w.sum(-1, keepdims=True)
         acc = acc + jnp.dot(
-            w.astype(jnp.bfloat16), packs[d, BLOCK : 2 * BLOCK, :],
+            w.astype(jnp.bfloat16), packs.at[d, 1].reshape(BLOCK, head_dim)[...],
             preferred_element_type=jnp.float32,
         )
         return total, acc
@@ -207,7 +259,14 @@
         total = partial[at, me_tensor].astype(jnp.float32)
         for hop in range(1, tensor):
             total = total + landed[at, hop].astype(jnp.float32)
-        out_ref[:, here] = (residual_ref[:, here].astype(jnp.float32) + total).astype(jnp.bfloat16)
+        for s in range(steps):
+            for block in range(per_tensor):
+                own = slice(block * nodes, (block + 1) * nodes)
+                at_row = block * pairs + s * nodes
+                out_ref[s, own, here] = (
+                    residual_ref[s, own, here].astype(jnp.float32)
+                    + total[at_row : at_row + nodes]
+                ).astype(jnp.bfloat16)
 
 
 def local(
@@ -221,64 +280,39 @@
     pairs = steps * nodes
     rows = pairs * head_count
     per_tensor = dp // tensor
-    pool_rows = pages * page * kv_local
-    new_rows = pairs * kv_local
     tile = min(512, columns)
     width = 1024
     chunks = prompt * kv_local // width
     bf16 = jnp.bfloat16
 
-    keys = prompt_kv[..., :head_dim].reshape(prompt * kv_local, head_dim)
-    values = prompt_kv[..., head_dim:].reshape(prompt * kv_local, head_dim)
-
-    at_page = jnp.arange(pages, dtype=jnp.int32)
-    match = page_table[:, :, None] == at_page
-    table_node = jnp.arange(nodes, dtype=jnp.int32)[:, None, None]
-    logical = jnp.arange(page_table.shape[1], dtype=jnp.int32)[None, :, None]
-    owner = jnp.where(match, table_node, 0).sum((0, 1))
-    filled = jnp.where(match, tail_len[:, None, None] - logical * page, 0).sum((0, 1))
-    live = jnp.arange(page, dtype=jnp.int32)[None, :] < filled[:, None]
-    node_row = jnp.where(live, owner[:, None], -1).astype(bf16)
-    node_row = jnp.repeat(node_row.reshape(-1), kv_local)
-    meta = jnp.broadcast_to(jnp.pad(node_row, (0, head_dim - pool_rows)), (16, head_dim))
-    spare = BLOCK - pool_rows - new_rows
-    pack = jnp.concatenate(
-        [
-            tail_pool[..., :head_dim].reshape(pool_rows, head_dim),
-            new_kv[..., :head_dim].reshape(new_rows, head_dim),
-            meta,
-            jnp.zeros((spare - 16, head_dim), bf16),
-            tail_pool[..., head_dim:].reshape(pool_rows, head_dim),
-            new_kv[..., head_dim:].reshape(new_rows, head_dim),
-            jnp.zeros((spare, head_dim), bf16),
-        ]
-    )
-    residual_rows = (
-        residual.reshape(steps, per_tensor, nodes, columns)
-        .transpose(1, 0, 2, 3)
-        .reshape(per_tensor * pairs, columns)
-    )
-
     dims = (dp, tensor, steps, nodes, head_count, kv_local, head_dim, pages, page, tile)
     vmem = pl.BlockSpec(memory_space=pltpu.VMEM)
     tiles = columns // tile
     dma = pltpu.SemaphoreType.DMA
-    out = pl.pallas_call(
+    return pl.pallas_call(
         functools.partial(kernel, dims),
-        out_shape=jax.ShapeDtypeStruct((per_tensor * pairs, columns), bf16),
-        in_specs=[vmem] * 5 + [pl.BlockSpec(memory_space=pl.ANY), vmem],
+        out_shape=jax.ShapeDtypeStruct(residual.shape, bf16),
+        in_specs=[pl.BlockSpec(memory_space=pltpu.SMEM)] * 2
+        + [vmem] * 3
+        + [pl.BlockSpec(memory_space=pltpu.HBM)] * 4,
         out_specs=vmem,
         scratch_shapes=[
             pltpu.VMEM((rows, head_dim), jnp.float32),
+            pltpu.VMEM((chunks, width // kv_local, kv_local, head_dim), bf16),
+            pltpu.VMEM((chunks, width // kv_local, kv_local, head_dim), bf16),
             pltpu.VMEM((chunks, rows, width), jnp.float32),
             pltpu.VMEM((dp, rows, BLOCK), jnp.float32),
-            pltpu.VMEM((dp, 2 * BLOCK, head_dim), bf16),
+            pltpu.VMEM((dp, 2, BLOCK // kv_local, kv_local, head_dim), bf16),
+            pltpu.VMEM((dp, 16, BLOCK), bf16),
             pltpu.VMEM(out_weight.shape, bf16),
             pltpu.VMEM((dp, pairs, head_count * head_dim), bf16),
             pltpu.VMEM((tiles, tensor, per_tensor * pairs, tile), bf16),
             pltpu.VMEM((tiles, tensor, per_tensor * pairs, tile), bf16),
             dma,
-            dma,
+            dma((2, 2)),
+            dma((2, chunks)),
+            dma((dp,)),
+            dma((dp,)),
             dma((dp,)),
             dma((dp,)),
             dma((dp,)),
@@ -287,15 +321,18 @@
             dma((tiles, tensor)),
         ],
         compiler_params=pltpu.CompilerParams(
-            collective_id=0, has_side_effects=True, vmem_limit_bytes=48 * 1024 * 1024
+            collective_id=0, has_side_effects=True, vmem_limit_bytes=63 * 1024 * 1024
         ),
     )(
-        query.reshape(rows, head_dim), keys, values, pack, fork_parent, out_weight, residual_rows
-    )
-    return (
-        out.reshape(per_tensor, steps, nodes, columns)
-        .transpose(1, 0, 2, 3)
-        .reshape(residual.shape)
+        page_table.T,
+        tail_len,
+        query.reshape(rows, head_dim),
+        fork_parent,
+        residual,
+        prompt_kv,
+        tail_pool.reshape(pages * page, kv_local, 2 * head_dim),
+        new_kv.reshape(pairs, kv_local, 2 * head_dim),
+        out_weight,
     )
 
 

time: 31.9 us -> 27.6 us (0.87)
  local copies, waits for them, and re-layouts: 6.09 us -> 1.49 us
  Pallas kernels: 23.9 us -> 25.9 us
  other arithmetic: 1.57 us -> 0 us
    slice x3 -> x0, local copies, waits for them, and re-layouts: 4.21 us -> none  [the longest x1 2.71 us: local(): values = prompt_kv[..., head_dim:].reshape(prompt * kv_local, head_dim)]
    pallas_call x1, Pallas kernels: 23.9 us -> 25.9 us  [local(): pl.pallas_call(functools.partial(kernel, dims), out_shape=jax.ShapeDtypeS...]
    another operation x2 -> x0, local copies, waits for them, and re-layouts: 1.52 us -> none  [the longest x1 0.86 us: local(): residual_rows = residual.reshape(steps, per_tensor, nodes, columns).trans...]
    unnamed x10 -> x1, local copies, waits for them, and re-layouts: 0.06 us -> 1.49 us
    reduce_sum x1 -> x0, other arithmetic: 0.77 us -> none  [local(): jnp.where(match, tail_len[:, None, None] - logical * page, 0).sum((0, 1))]
    sub x1 -> x0, other arithmetic: 0.72 us -> none  [local(): tail_len[:, None, None] - logical * page]
where the time goes in v2:
time: 27.6 us; the launch traced here: 27.4 us
  Pallas kernels  25.9 us (94%)
  local copies, waits for them, and re-layouts  1.49 us (5%)
    pallas_call x1, Pallas kernels, local(): pl.pallas_call(functools.partial(kernel, dims), out_shape=jax.ShapeDtypeS...  25.9 us
    unnamed x1, local copies, waits for them, and re-layouts  1.49 us

profile of v2, /device:TPU:0, one launch (start us, length us, event | category | flops | bytes accessed | tf_op | source)
XLA Modules:
  0.0 27.4 jit_solution(4937897280772436470)
XLA Ops:
  0.0 25.9 %shard_map.91 = bf16[4,4,2048]{2,1,0:T(4,128)(2,1)} custom-call(s32[2,4]{1,0:T(2,128)} %bitcast.7, s32[4]{0:T(128)} %len_ref.1, bf16[256,128]{1,0:T(8,128)(2,1)} %bitcast.4, s32[4,16]{1,0:T(4,128)} %fork_ref.1, bf16[4,4,2048]{2,1,0:T(4,128)(2,1)} %residual_ref.1, bf16[2048,2,256]{2,1,0:T(2,128)(2,1)} %prompt_ref.1, bf16[32,2,256]{2,1,0:T(2,128)(2,1)} %bitcast.5, ...), custom_call_target="tpu_custom_call" | custom-call | tf_op jit(solution)/shard_map/pallas_call | solution.py:292
  25.9 1.5 %copy.11 = bf16[4,4,2048]{2,1,0:T(4,128)(2,1)} copy(bf16[4,4,2048]{2,1,0:T(4,128)(2,1)} %shard_map.91) | data formatting | bytes 131072

commit v3 on v2

--- a/solution.py
+++ b/solution.py
@@ -10,14 +10,16 @@
 
 MESH = pl.DeviceIdType.MESH
 BLOCK = 128
+TAIL_WIDTH = 256
 
 
 def kernel(
-    dims, table_ref, len_ref, q_ref, fork_ref, residual_ref, prompt_ref, pool_ref, new_ref,
+    dims, table_in, len_in, q_in, fork_in, residual_in, pool_in, prompt_ref, new_ref,
     weight_ref, out_ref,
+    table_ref, len_ref, q_ref, fork_ref, residual_ref, pool_ref,
     q_flat, prompt_keys, prompt_values, scores, tail_scores, packs, owners, weight, heads,
     partial, landed,
-    weight_sem, own_sem, prompt_sem, pack_send, pack_recv, owner_send, owner_recv,
+    in_sem, weight_sem, own_sem, prompt_sem, pack_send, pack_recv, owner_send, owner_recv,
     head_send, head_recv, part_send, part_recv,
 ):
     dp, tensor, steps, nodes, head_count, kv_local, head_dim, pages, page, tile = dims
@@ -31,24 +33,31 @@
     factor = head_dim ** (-0.5) * math.log2(math.e)
 
     total_chunks, chunk_prompt = prompt_keys.shape[0], prompt_keys.shape[1]
-    pool_tokens = pages * page
-    half = BLOCK // kv_local
-
+    pool_tokens = nodes * page
+    span = (pool_tokens + pairs) * kv_local
+    join = TAIL_WIDTH // span
+
+    small_copies = [
+        pltpu.make_async_copy(source, target, in_sem.at[at])
+        for at, (source, target) in enumerate(
+            (
+                (table_in, table_ref), (len_in, len_ref), (pool_in, pool_ref), (q_in, q_ref),
+                (fork_in, fork_ref), (residual_in, residual_ref),
+            )
+        )
+    ]
+    for copy in small_copies[:3]:
+        copy.start()
     own_copies = []
     for part in range(2):
         lanes = slice(part * head_dim, (part + 1) * head_dim)
         own_copies.append(
             pltpu.make_async_copy(
-                pool_ref.at[:, :, lanes], packs.at[me, part, 0:pool_tokens], own_sem.at[part, 0]
+                new_ref.at[:, :, lanes], packs.at[part, me, pool_tokens : pool_tokens + pairs],
+                own_sem.at[part],
             )
         )
-        own_copies.append(
-            pltpu.make_async_copy(
-                new_ref.at[:, :, lanes], packs.at[me, part, pool_tokens : pool_tokens + pairs],
-                own_sem.at[part, 1],
-            )
-        )
-    for copy in own_copies:
+    for copy in own_copies + small_copies[3:]:
         copy.start()
 
     def prompt_copy(c, part):
@@ -78,18 +87,20 @@
             device_id_type=MESH,
         )
 
-    spot = lax.broadcasted_iota(jnp.int32, (16, BLOCK), 1) // kv_local
-    owner = jnp.full((16, BLOCK), -1.0, jnp.float32)
+    for copy in small_copies[:3]:
+        copy.wait()
+    lane = lax.broadcasted_iota(jnp.int32, (16, BLOCK), 1)
+    spot = lane % span // kv_local
+    owner = (spot - pool_tokens) % nodes
     for n in range(nodes):
-        for j in range(pages // nodes):
-            held = (spot // page == table_ref[j, n]) & (spot % page + j * page < len_ref[n])
-            owner = jnp.where(held & (spot < pool_tokens), float(n), owner)
-    owners[me] = owner.astype(jnp.bfloat16)
-    used = pool_tokens + pairs
-    for part in range(2):
-        packs[me, part, used:half] = jnp.zeros(
-            (half - used, kv_local, head_dim), jnp.bfloat16
-        )
+        owner = jnp.where(
+            spot // page == n, jnp.where(spot % page < len_ref[n], n, -1 - me * nodes), owner
+        )
+        for part in range(2):
+            lanes = slice(part * head_dim, (part + 1) * head_dim)
+            packs[part, me, n * page : (n + 1) * page] = pool_ref[table_ref[0, n], :, :, lanes]
+    owner = jnp.where(lane // span == me % (BLOCK // span), owner + me * nodes, -1)
+    owners[me] = owner.astype(jnp.float32).astype(jnp.bfloat16)
     for copy in own_copies:
         copy.wait()
     pl.semaphore_wait(barrier, dp + tensor - 2)
@@ -97,19 +108,23 @@
     pack_copies = []
     for hop in range(1, dp):
         for buffer, send, recv in (
-            (packs, pack_send, pack_recv), (owners, owner_send, owner_recv)
+            (owners.at[me], owner_send.at[hop], owner_recv.at[hop]),
+            (packs.at[0, me], pack_send.at[0, hop], pack_recv.at[0, hop]),
+            (packs.at[1, me], pack_send.at[1, hop], pack_recv.at[1, hop]),
         ):
             copy = pltpu.make_async_remote_copy(
-                src_ref=buffer.at[me],
-                dst_ref=buffer.at[me],
-                send_sem=send.at[hop],
-                recv_sem=recv.at[hop],
+                src_ref=buffer,
+                dst_ref=buffer,
+                send_sem=send,
+                recv_sem=recv,
                 device_id={"dp": lax.rem(me + hop, dp)},
                 device_id_type=MESH,
             )
             copy.start()
             pack_copies.append(copy)
 
+    for copy in small_copies[3:]:
+        copy.wait()
     q_flat[...] = q_ref[...].astype(jnp.float32)
     q = jnp.concatenate(
         [q_flat[pl.ds(h, pairs, stride=head_count), :] for h in range(head_count)], axis=0
@@ -165,38 +180,43 @@
         parent = jnp.where(parent >= 0.0, parent, ids)
         found = jnp.where(ids == current, parent, 0.0).sum(-1, keepdims=True)
         current = jnp.where(reached, found, current)
-    lane = lax.broadcasted_iota(jnp.int32, (pairs, BLOCK), 1)
-    wanted = jnp.broadcast_to(current, (pairs, BLOCK))
+    lane = lax.broadcasted_iota(jnp.int32, (pairs, TAIL_WIDTH), 1)
+    spot = lane % span // kv_local
+    wanted = jnp.broadcast_to(current, (pairs, TAIL_WIDTH))
     for step in range(steps):
-        wanted = jnp.where(
-            lane >= pool_rows + step * nodes * kv_local, places[step], wanted
-        )
-    is_new = lane >= pool_rows
-    new_node = ((lane - pool_rows) // kv_local % nodes).astype(jnp.float32)
-    inside = lane < pool_rows + new_rows
+        wanted = jnp.where(spot >= pool_tokens + step * nodes, places[step], wanted)
     parity = lane % kv_local
+    reachable = wanted >= 0.0
 
     for copy in pack_copies:
         copy.wait()
+
+    def tail_keys(part, d):
+        return packs.at[part, pl.ds(d * join, join)].reshape(TAIL_WIDTH, head_dim)[...]
 
     def tail_score(d, highest):
         s = lax.dot_general(
-            q, packs.at[d, 0].reshape(BLOCK, head_dim)[...], contract, preferred_element_type=jnp.float32
-        )
-        node = owners[d].astype(jnp.float32)
-        node = jnp.where(is_new, new_node, jnp.broadcast_to(node[0:1, :], (pairs, BLOCK)))
-        base = (d * nodes).astype(jnp.float32)
-        seen = inside & (node >= 0.0) & (node + base == wanted)
+            q, tail_keys(0, d), contract, preferred_element_type=jnp.float32
+        )
+        per_block = BLOCK // span
+        blocks = []
+        for first in range(0, join, per_block):
+            node = owners[d * join + first].astype(jnp.float32)
+            for more in range(first + 1, first + per_block):
+                node = jnp.maximum(node, owners[d * join + more].astype(jnp.float32))
+            blocks.append(node)
+        node = jnp.concatenate(blocks, axis=1)[0:1, :]
+        seen = reachable & (node == wanted)
         pieces = []
         for k in range(kv_local):
             keep = (seen & (parity == k))[None]
-            part = s[k * group * pairs : (k + 1) * group * pairs].reshape(group, pairs, BLOCK)
-            pieces.append(jnp.where(keep, part, -jnp.inf).reshape(group * pairs, BLOCK))
+            part = s[k * group * pairs : (k + 1) * group * pairs].reshape(group, pairs, TAIL_WIDTH)
+            pieces.append(jnp.where(keep, part, -jnp.inf).reshape(group * pairs, TAIL_WIDTH))
         s = jnp.concatenate(pieces, axis=0)
         tail_scores[d] = s
         return jnp.maximum(highest, s.max(-1, keepdims=True))
 
-    highest = lax.fori_loop(0, dp, tail_score, prompt_max)
+    highest = lax.fori_loop(0, dp // join, tail_score, prompt_max)
     carried = jnp.exp2((prompt_max - highest) * factor)
 
     def tail_weigh(d, carry):
@@ -204,13 +224,13 @@
         w = jnp.exp2((tail_scores[d] - highest) * factor)
         total = total + w.sum(-1, keepdims=True)
         acc = acc + jnp.dot(
-            w.astype(jnp.bfloat16), packs.at[d, 1].reshape(BLOCK, head_dim)[...],
+            w.astype(jnp.bfloat16), tail_keys(1, d),
             preferred_element_type=jnp.float32,
         )
         return total, acc
 
     denominator, mixed = lax.fori_loop(
-        0, dp, tail_weigh, (prompt_sum * carried, prompt_acc * carried)
+        0, dp // join, tail_weigh, (prompt_sum * carried, prompt_acc * carried)
     )
     attended = (mixed / denominator).astype(jnp.bfloat16)
     for h in range(head_count):
@@ -280,6 +300,7 @@
     pairs = steps * nodes
     rows = pairs * head_count
     per_tensor = dp // tensor
+    span = (nodes * page + pairs) * kv_local
     tile = min(512, columns)
     width = 1024
     chunks = prompt * kv_local // width
@@ -292,27 +313,32 @@
     return pl.pallas_call(
         functools.partial(kernel, dims),
         out_shape=jax.ShapeDtypeStruct(residual.shape, bf16),
-        in_specs=[pl.BlockSpec(memory_space=pltpu.SMEM)] * 2
-        + [vmem] * 3
-        + [pl.BlockSpec(memory_space=pltpu.HBM)] * 4,
+        in_specs=[pl.BlockSpec(memory_space=pltpu.HBM)] * 9,
         out_specs=vmem,
         scratch_shapes=[
+            pltpu.SMEM(page_table.shape[::-1], jnp.int32),
+            pltpu.SMEM(tail_len.shape, jnp.int32),
+            pltpu.VMEM((rows, head_dim), bf16),
+            pltpu.VMEM(fork_parent.shape, jnp.int32),
+            pltpu.VMEM(residual.shape, bf16),
+            pltpu.VMEM(tail_pool.shape, bf16),
             pltpu.VMEM((rows, head_dim), jnp.float32),
             pltpu.VMEM((chunks, width // kv_local, kv_local, head_dim), bf16),
             pltpu.VMEM((chunks, width // kv_local, kv_local, head_dim), bf16),
             pltpu.VMEM((chunks, rows, width), jnp.float32),
-            pltpu.VMEM((dp, rows, BLOCK), jnp.float32),
-            pltpu.VMEM((dp, 2, BLOCK // kv_local, kv_local, head_dim), bf16),
+            pltpu.VMEM((dp * span // TAIL_WIDTH, rows, TAIL_WIDTH), jnp.float32),
+            pltpu.VMEM((2, dp, span // kv_local, kv_local, head_dim), bf16),
             pltpu.VMEM((dp, 16, BLOCK), bf16),
             pltpu.VMEM(out_weight.shape, bf16),
             pltpu.VMEM((dp, pairs, head_count * head_dim), bf16),
             pltpu.VMEM((tiles, tensor, per_tensor * pairs, tile), bf16),
             pltpu.VMEM((tiles, tensor, per_tensor * pairs, tile), bf16),
+            dma((6,)),
             dma,
-            dma((2, 2)),
+            dma((2,)),
             dma((2, chunks)),
-            dma((dp,)),
-            dma((dp,)),
+            dma((2, dp)),
+            dma((2, dp)),
             dma((dp,)),
             dma((dp,)),
             dma((dp,)),
@@ -329,8 +355,8 @@
         query.reshape(rows, head_dim),
         fork_parent,
         residual,
+        tail_pool,
         prompt_kv,
-        tail_pool.reshape(pages * page, kv_local, 2 * head_dim),
         new_kv.reshape(pairs, kv_local, 2 * head_dim),
         out_weight,
     )

time: 27.6 us -> 23.7 us (0.86)
  Pallas kernels: 25.9 us -> 22.1 us
    pallas_call x1, Pallas kernels: 25.9 us -> 22.1 us  [local(): pl.pallas_call(functools.partial(kernel, dims), out_shape=jax.ShapeDtypeS...]
where the time goes in v3:
time: 23.7 us; the launch traced here: 23.6 us
  Pallas kernels  22.1 us (93%)
  local copies, waits for them, and re-layouts  1.49 us (6%)
    pallas_call x1, Pallas kernels, local(): pl.pallas_call(functools.partial(kernel, dims), out_shape=jax.ShapeDtypeS...  22.1 us
    unnamed x1, local copies, waits for them, and re-layouts  1.49 us

profile of v3, /device:TPU:0, one launch (start us, length us, event | category | flops | bytes accessed | tf_op | source)
XLA Modules:
  0.0 23.6 jit_solution(2250896050899808099)
XLA Ops:
  0.0 22.1 %shard_map.91 = bf16[4,4,2048]{2,1,0:T(4,128)(2,1)} custom-call(s32[2,4]{1,0:T(2,128)} %bitcast.5, s32[4]{0:T(128)} %len_in.1, bf16[256,128]{1,0:T(8,128)(2,1)} %bitcast.3, s32[4,16]{1,0:T(4,128)} %fork_in.1, bf16[4,4,2048]{2,1,0:T(4,128)(2,1)} %residual_in.1, bf16[8,4,2,256]{3,2,1,0:T(2,128)(2,1)} %pool_in.1, bf16[2048,2,256]{2,1,0:T(2,128)(2,1)} %prompt_ref.1, ...), custom_call_target="tpu_custom_call" | custom-call | tf_op jit(solution)/shard_map/pallas_call | solution.py:313
  22.1 1.5 %copy.11 = bf16[4,4,2048]{2,1,0:T(4,128)(2,1)} copy(bf16[4,4,2048]{2,1,0:T(4,128)(2,1)} %shard_map.91) | data formatting | bytes 131072

commit v4 on v3

--- a/solution.py
+++ b/solution.py
@@ -312,7 +312,7 @@
     dma = pltpu.SemaphoreType.DMA
     return pl.pallas_call(
         functools.partial(kernel, dims),
-        out_shape=jax.ShapeDtypeStruct(residual.shape, bf16),
+        out_shape=pltpu.VMEM(residual.shape, bf16),
         in_specs=[pl.BlockSpec(memory_space=pltpu.HBM)] * 9,
         out_specs=vmem,
         scratch_shapes=[

time: 23.7 us -> 22.2 us (0.937)
  local copies, waits for them, and re-layouts: 1.49 us -> 0.63 us
  Pallas kernels: 22.1 us -> 21.5 us
    unnamed x1, local copies, waits for them, and re-layouts: 1.49 us -> 0.63 us
    pallas_call x1, Pallas kernels: 22.1 us -> 21.5 us  [local(): pl.pallas_call(functools.partial(kernel, dims), out_shape=pltpu.VMEM(resi...]
where the time goes in v4:
time: 22.2 us; the launch traced here: 22.1 us
  Pallas kernels  21.5 us (97%)
  local copies, waits for them, and re-layouts  0.63 us (3%)
    pallas_call x1, Pallas kernels, local(): pl.pallas_call(functools.partial(kernel, dims), out_shape=pltpu.VMEM(resi...  21.5 us
    unnamed x1, local copies, waits for them, and re-layouts  0.63 us

profile of v4, /device:TPU:0, one launch (start us, length us, event | category | flops | bytes accessed | tf_op | source)
XLA Modules:
  0.0 22.1 jit_solution(3893871212474320427)
XLA Ops:
  0.0 21.5 %shard_map.91 = bf16[4,4,2048]{2,1,0:T(4,128)(2,1)S(1)} custom-call(s32[2,4]{1,0:T(2,128)} %bitcast.5, s32[4]{0:T(128)} %len_in.1, bf16[256,128]{1,0:T(8,128)(2,1)} %bitcast.3, s32[4,16]{1,0:T(4,128)} %fork_in.1, bf16[4,4,2048]{2,1,0:T(4,128)(2,1)} %residual_in.1, bf16[8,4,2,256]{3,2,1,0:T(2,128)(2,1)} %pool_in.1, bf16[2048,2,256]{2,1,0:T(2,128)(2,1)} %prompt_ref.1, ...), custom_call_target="tpu_custom_call" | custom-call | tf_op jit(solution)/shard_map/pallas_call | solution.py:313
  21.5 0.6 %copy.11 = bf16[4,4,2048]{2,1,0:T(4,128)(2,1)} copy(bf16[4,4,2048]{2,1,0:T(4,128)(2,1)S(1)} %shard_map.91) | data formatting | bytes 131072

commit v5 on v4

--- a/solution.py
+++ b/solution.py
@@ -236,6 +236,14 @@
     for h in range(head_count):
         heads[me, :, h * head_dim : (h + 1) * head_dim] = attended[h * pairs : (h + 1) * pairs]
 
+    def partner(index, hop):
+        bit = 1
+        while bit <= hop:
+            if hop & bit:
+                index = index + bit - 2 * bit * (index // bit % 2)
+            bit *= 2
+        return index
+
     head_copies = []
     for hop in range(1, dp):
         copy = pltpu.make_async_remote_copy(
@@ -243,42 +251,55 @@
             dst_ref=heads.at[me],
             send_sem=head_send.at[hop],
             recv_sem=head_recv.at[hop],
-            device_id={"dp": lax.rem(me + hop, dp)},
+            device_id={"dp": partner(me, hop)},
             device_id_type=MESH,
         )
         copy.start()
         head_copies.append(copy)
     weight_copy.wait()
-    for copy in head_copies:
-        copy.wait()
 
     columns = weight.shape[1]
     per_tensor = dp // tensor
-    gathered = heads[...].reshape(dp * pairs, head_count * head_dim)
-    part_copies = []
+
+    def part_copy(at, hop):
+        peer = lax.rem(me_tensor + hop, tensor)
+        return pltpu.make_async_remote_copy(
+            src_ref=partial.at[peer, at],
+            dst_ref=landed.at[hop, at],
+            send_sem=part_send.at[hop, at],
+            recv_sem=part_recv.at[hop, at],
+            device_id={"tensor": peer},
+            device_id_type=MESH,
+        )
+
+    for turn in range(0, tensor, 2):
+        block = partner(me // per_tensor, turn) // 2 * 2
+        for hop in range(max(1, turn * per_tensor), (turn + 2) * per_tensor):
+            head_copies[hop - 1].wait_recv()
+        gathered = heads[pl.ds(block * per_tensor, 2 * per_tensor)].reshape(
+            2 * per_tensor * pairs, head_count * head_dim
+        )
+        for at in range(columns // tile):
+            here = slice(at * tile, (at + 1) * tile)
+            product = jnp.dot(gathered, weight[:, here], preferred_element_type=jnp.float32)
+            product = product.astype(jnp.bfloat16)
+            partial[block, at] = product[: per_tensor * pairs]
+            partial[block + 1, at] = product[per_tensor * pairs :]
+            for hop in range(1, tensor):
+
+                @pl.when(lax.rem(me_tensor + hop, tensor) // 2 == block // 2)
+                def _():
+                    part_copy(at, hop).start()
+
+    for copy in head_copies:
+        copy.wait_send()
     for at in range(columns // tile):
         here = slice(at * tile, (at + 1) * tile)
-        product = jnp.dot(gathered, weight[:, here], preferred_element_type=jnp.float32)
-        partial[at] = product.astype(jnp.bfloat16).reshape(tensor, per_tensor * pairs, tile)
         for hop in range(1, tensor):
-            peer = lax.rem(me_tensor + hop, tensor)
-            copy = pltpu.make_async_remote_copy(
-                src_ref=partial.at[at, peer],
-                dst_ref=landed.at[at, hop],
-                send_sem=part_send.at[at, hop],
-                recv_sem=part_recv.at[at, hop],
-                device_id={"tensor": peer},
-                device_id_type=MESH,
-            )
-            copy.start()
-            part_copies.append(copy)
-    for at in range(columns // tile):
-        here = slice(at * tile, (at + 1) * tile)
-        for copy in part_copies[at * (tensor - 1) : (at + 1) * (tensor - 1)]:
-            copy.wait()
-        total = partial[at, me_tensor].astype(jnp.float32)
+            part_copy(at, hop).wait()
+        total = partial[me_tensor, at].astype(jnp.float32)
         for hop in range(1, tensor):
-            total = total + landed[at, hop].astype(jnp.float32)
+            total = total + landed[hop, at].astype(jnp.float32)
         for s in range(steps):
             for block in range(per_tensor):
                 own = slice(block * nodes, (block + 1) * nodes)
@@ -331,8 +352,8 @@
             pltpu.VMEM((dp, 16, BLOCK), bf16),
             pltpu.VMEM(out_weight.shape, bf16),
             pltpu.VMEM((dp, pairs, head_count * head_dim), bf16),
-            pltpu.VMEM((tiles, tensor, per_tensor * pairs, tile), bf16),
-            pltpu.VMEM((tiles, tensor, per_tensor * pairs, tile), bf16),
+            pltpu.VMEM((tensor, tiles, per_tensor * pairs, tile), bf16),
+            pltpu.VMEM((tensor, tiles, per_tensor * pairs, tile), bf16),
             dma((6,)),
             dma,
             dma((2,)),
@@ -343,8 +364,8 @@
             dma((dp,)),
             dma((dp,)),
             dma((dp,)),
-            dma((tiles, tensor)),
-            dma((tiles, tensor)),
+            dma((tensor, tiles)),
+            dma((tensor, tiles)),
         ],
         compiler_params=pltpu.CompilerParams(
             collective_id=0, has_side_effects=True, vmem_limit_bytes=63 * 1024 * 1024

time: 22.2 us -> 21.4 us (0.964)
  Pallas kernels: 21.5 us -> 20.7 us
    pallas_call x1, Pallas kernels: 21.5 us -> 20.7 us  [local(): pl.pallas_call(functools.partial(kernel, dims), out_shape=pltpu.VMEM(resi...]
where the time goes in v5:
time: 21.4 us; the launch traced here: 21.3 us
  Pallas kernels  20.7 us (97%)
  local copies, waits for them, and re-layouts  0.63 us (3%)
    pallas_call x1, Pallas kernels, local(): pl.pallas_call(functools.partial(kernel, dims), out_shape=pltpu.VMEM(resi...  20.7 us
    unnamed x1, local copies, waits for them, and re-layouts  0.63 us

profile of v5, /device:TPU:0, one launch (start us, length us, event | category | flops | bytes accessed | tf_op | source)
XLA Modules:
  0.0 21.3 jit_solution(6790462549776820414)
XLA Ops:
  0.0 20.7 %shard_map.91 = bf16[4,4,2048]{2,1,0:T(4,128)(2,1)S(1)} custom-call(s32[2,4]{1,0:T(2,128)} %bitcast.5, s32[4]{0:T(128)} %len_in.1, bf16[256,128]{1,0:T(8,128)(2,1)} %bitcast.3, s32[4,16]{1,0:T(4,128)} %fork_in.1, bf16[4,4,2048]{2,1,0:T(4,128)(2,1)} %residual_in.1, bf16[8,4,2,256]{3,2,1,0:T(2,128)(2,1)} %pool_in.1, bf16[2048,2,256]{2,1,0:T(2,128)(2,1)} %prompt_ref.1, ...), custom_call_target="tpu_custom_call" | custom-call | tf_op jit(solution)/shard_map/pallas_call | solution.py:334
  20.7 0.6 %copy.11 = bf16[4,4,2048]{2,1,0:T(4,128)(2,1)} copy(bf16[4,4,2048]{2,1,0:T(4,128)(2,1)S(1)} %shard_map.91) | data formatting | bytes 131072
